TPU v7x, 256 devices: a whole 4x4x8 slice. The times are simulated.
256 devices in a mesh: side: 2 (over core), col: 32 (over z, y), hid: 4 (over x).
Axes of the slice: x: 4, y: 4, z: 8, core: 2. Of those that a mesh axis runs over, the one named last changes fastest.
Arguments:
- residual: bfloat16 [4096, 4096], P(('side', 'col', 'hid')), may hold values from -6 to 6
- queries: bfloat16 [4096, 4096], P(('side', 'col', 'hid')), may hold values from -37 to 37
- key_values: bfloat16 [4096, 256, 256], P(('side', 'col', 'hid')), may hold values from -13 to 13
- lengths: int32 [4096], P(('side', 'col', 'hid')), may hold values from 2 to 256, as said below
- route_ids: int32 [4096, 3], P(('side', 'col', 'hid')), may hold values from 0 to 31, all different within a row; in each aligned block of 16 rows (0 to 15, 16 to 31, ...) at most 2 rows name the same one
- route_weights: float32 [4096, 3], P(('side', 'col', 'hid')), may hold values from 0.1 to 1
- norm_gain: float32 [4096], replicated, may hold values from 0.1 to 1.9
- w_gate_up: bfloat16 [32, 4096, 2, 3072], P('col', None, None, ('side', 'hid')), may hold values from -0.09375 to 0.09375
- w_down: bfloat16 [32, 3072, 4096], P('col', ('side', 'hid')), may hold values from -0.109375 to 0.109375
Outputs:
- mixed: bfloat16 [4096, 4096], P(('side', 'col', 'hid'))
Inputs may be any that keep to these rules, and one draw needn't show every extreme that they name: `lengths`: the live positions of a row are its first ones; some row has exactly 256. `route_ids`: a row names 3 different experts; among the rows of one device no expert is named more than 2 times, and one is named exactly 2 times.
All inputs are finite; a program needn't handle non-finite values.
Results may differ from a plain program's by a relative error of at most 0.0052.
Values may be sent and summed in bfloat16 or wider, within the bound.
A program may use at most 128 MiB of HBM per device.

v0:
```python
import math

import jax
import jax.numpy as jnp
from jax import lax
from jax.sharding import PartitionSpec as P

HEADS = 32
HD = 128


def on_device(
    residual, queries, key_values, lengths, route_ids, route_weights, norm_gain, w_gate_up, w_down
):
    row_count, width = residual.shape
    heads_q = queries.reshape(row_count, HEADS, HD)
    key_rows = key_values[:, :, :HD]
    value_rows = key_values[:, :, HD:]
    scores = jnp.einsum("rhd,rtd->rht", heads_q, key_rows, preferred_element_type=jnp.float32) * (
        1.0 / math.sqrt(HD)
    )
    positions = jnp.arange(key_values.shape[1], dtype=jnp.int32)
    visible = positions[None, None, :] < lengths[:, None, None]
    scores = jnp.where(visible, scores, -1e30)
    row_peak = jnp.max(scores, axis=2, keepdims=True)
    exponent = jnp.where(visible, jnp.exp(scores - row_peak), 0.0)
    normalized = (exponent / jnp.sum(exponent, axis=2, keepdims=True)).astype(jnp.bfloat16)
    attended = jnp.einsum(
        "rht,rtd->rhd", normalized, value_rows, preferred_element_type=jnp.float32
    ).reshape(row_count, width)
    hidden_state = residual.astype(jnp.float32) + attended
    mean_square = jnp.mean(hidden_state * hidden_state, axis=1, keepdims=True)
    normed = (hidden_state * lax.rsqrt(mean_square + 1e-06) * norm_gain[None, :]).astype(
        jnp.bfloat16
    )
    columns = lax.axis_size("col")
    group = lax.axis_size(("side", "hid"))
    fanout = route_ids.shape[1]
    slot_count = max(2, (row_count * fanout + columns - 1) // columns)
    flat_ids = route_ids.reshape(-1)
    one_hot = (flat_ids[:, None] == jnp.arange(columns, dtype=jnp.int32)[None, :]).astype(jnp.int32)
    earlier = jnp.cumsum(one_hot, axis=0) - one_hot
    slot_index = jnp.sum(earlier * one_hot, axis=1)
    position = flat_ids * slot_count + slot_index
    slot_ids = jnp.arange(columns * slot_count, dtype=jnp.int32)
    selector = (slot_ids[:, None] == position[None, :]).astype(jnp.bfloat16)
    selector = jnp.sum(selector.reshape(columns * slot_count, row_count, fanout), axis=2)
    dispatch = jnp.dot(selector, normed, preferred_element_type=jnp.float32).astype(jnp.bfloat16)
    dispatch = dispatch.reshape(columns, slot_count, width)
    joined = w_gate_up[0].reshape(width, -1)
    half_cols = joined.shape[1] // 2
    grouped = lax.all_gather(dispatch[None], ("side", "hid"), axis=0, tiled=True)
    arrived = lax.all_to_all(grouped, "col", split_axis=1, concat_axis=1, tiled=True)
    rows_in = arrived.reshape(-1, width)
    both_parts = jnp.dot(rows_in, joined, preferred_element_type=jnp.float32)
    activ = (jax.nn.silu(both_parts[:, :half_cols]) * both_parts[:, half_cols:]).astype(
        jnp.bfloat16
    )
    share = activ.shape[0] // group
    down_matrix = w_down[0]
    partial_out = jnp.dot(activ, down_matrix, preferred_element_type=jnp.float32)
    summed = lax.psum(partial_out, ("side", "hid"))
    share_rows = lax.dynamic_slice_in_dim(summed, lax.axis_index(("side", "hid")) * share, share, 0)
    expert_out = share_rows.astype(jnp.bfloat16).reshape(columns, slot_count, width)
    returned = lax.all_to_all(expert_out, "col", split_axis=0, concat_axis=0, tiled=True).reshape(
        columns * slot_count, width
    )
    picked = (
        jnp.take(returned, position, axis=0).reshape(row_count, fanout, width).astype(jnp.float32)
    )
    moe_sum = jnp.sum(route_weights[:, :, None] * picked, axis=1)
    return (hidden_state + moe_sum).astype(jnp.bfloat16)


def solution(mesh):
    placed = (
        P(("side", "col", "hid"), None),
        P(("side", "col", "hid"), None),
        P(("side", "col", "hid"), None, None),
        P(("side", "col", "hid")),
        P(("side", "col", "hid"), None),
        P(("side", "col", "hid"), None),
        P(),
        P("col", None, None, ("side", "hid")),
        P("col", ("side", "hid"), None),
    )
    return jax.shard_map(
        on_device,
        mesh=mesh,
        in_specs=placed,
        out_specs=P(("side", "col", "hid"), None),
        check_vma=False,
    )
```

profile of v0, /device:TPU:2, one launch (start us, length us, event | category | flops | bytes accessed | tf_op | source)
XLA Modules:
  0.0 424.3 jit_solution(6993928507952184325)
XLA Ops:
  6.5 0.0 copy-start
  6.5 0.0 all-gather.2.cloned.1.call-start
  6.5 0.9 iota_compare_fusion.2
  7.4 1.1 copy.34
  8.5 1.7 fusion.4
  10.2 0.0 copy-start.2
  10.2 0.8 copy-done.2
  11.0 0.8 fusion.25
  11.8 2.5 fusion.7
  14.3 0.0 copy-done.1
  14.4 0.3 multiply_reduce_fusion.1
  14.6 0.6 add_rsqrt_fusion
  15.2 0.1 copy.28
  15.3 0.1 reshape.113
  15.4 0.7 fusion.16
  16.1 1.4 reduce_window_sum.11
  17.5 0.9 select_reduce_fusion
  18.4 0.6 copy-done.4
  19.0 0.7 reduce_sum.54
  19.7 1.3 compare_and_fusion
  21.0 0.7 copy.30
  21.6 0.8 fusion.18
  22.4 1.9 convolution_convert_fusion
  24.3 2.2 broadcast_in_dim_reshape.4
  26.4 2.1 copy.31
  28.6 0.0 all-gather.2.cloned.1.call-update
  28.6 36.7 %all-gather.2.cloned.1.call-done = bf16[8,32,2,4096]{3,1,2,0:T(8,128)(2,1)} async-done(((bf16[1,32,2,4096]{3,1,2,0:T(8,128)(2,1)}), bf16[8,32,2,4096]{3,1,2,0:T(8,128)(2,1)}) %all-gather.2.cloned.1.call-update) | async-done | bytes 4194320 | tf_op jit(solution)/shard_map/all_gather | solution.py:52
  65.3 8.6 %copy.32 = bf16[8,32,2,4096]{3,2,0,1:T(2,128)(2,1)} copy(bf16[8,32,2,4096]{3,1,2,0:T(8,128)(2,1)} %all-gather.2.cloned.1.call-done) | data formatting | bytes 8388608 | tf_op jit(solution)/shard_map/all_gather | solution.py:52
  74.0 10.2 %all-to-all-start = ((bf16[8,32,2,4096]{3,2,0,1:T(2,128)(2,1)}), bf16[8,32,2,4096]{3,2,0,1:T(2,128)(2,1)}, u32[]{:S(2)}, u32[]{:S(2)}) async-start(bf16[8,32,2,4096]{3,2,0,1:T(2,128)(2,1)} %copy.32), calls=%async_computation | async-start | bytes 8388608 | tf_op jit(solution)/shard_map/all_to_all | solution.py:53
  84.2 6.5 %copy.36 = bf16[512,8,2,384]{3,1,2,0:T(8,128)(2,1)} copy(bf16[512,8,2,384]{3,2,1,0:T(2,128)(2,1)} %bitcast.30) | data formatting | bytes 12582912
  90.7 87.7 %all-to-all-done = bf16[8,32,2,4096]{3,2,0,1:T(2,128)(2,1)} async-done(((bf16[8,32,2,4096]{3,2,0,1:T(2,128)(2,1)}), bf16[8,32,2,4096]{3,2,0,1:T(2,128)(2,1)}, u32[]{:S(2)}, u32[]{:S(2)}) %all-to-all-start) | async-done | bytes 4194336 | tf_op jit(solution)/shard_map/all_to_all | solution.py:53
  178.4 10.1 %copy.33 = bf16[8,32,2,4096]{3,2,1,0:T(2,128)(2,1)} copy(bf16[8,32,2,4096]{3,2,0,1:T(2,128)(2,1)} %all-to-all-done) | data formatting | bytes 8388608 | tf_op jit(solution)/shard_map/all_to_all | solution.py:53
  188.4 7.2 %reshape.114 = bf16[512,4096]{1,0:T(8,128)(2,1)} reshape(bf16[8,32,2,4096]{3,2,1,0:T(2,128)(2,1)} %copy.33) | data formatting | bytes 8388608 | tf_op jit(solution)/shard_map/reshape | solution.py:54
  195.6 7.0 %fusion.26 = f32[512,768]{1,0:T(8,128)S(1)} fusion(bf16[512,4096]{1,0:T(8,128)(2,1)} %reshape.114, bf16[4096,768]{1,0:T(8,128)(2,1)} %bitcast.31), kind=kOutput, calls=%fused_computation.46 | convolution fusion | flops 3221225472 | bytes 12058624 | tf_op jit(solution)/shard_map/dot_general | solution.py:55
  202.7 5.6 %fusion.1 = f32[512,4096]{1,0:T(8,128)} fusion(bf16[1,384,4096]{2,1,0:T(8,128)(2,1)S(1)} %copy-done, f32[512,768]{1,0:T(8,128)S(1)} %fusion.26), kind=kOutput, calls=%fused_computation.3 | convolution fusion | flops 1611792384 | bytes 13107200 | tf_op jit(solution)/shard_map/dot_general | solution.py:61
  208.3 169.3 %all-reduce.1 = bf16[512,4096]{1,0:T(8,128)(2,1)} all-reduce(f32[512,4096]{1,0:T(8,128)} %fusion.1), channel_id=1, replica_groups=mesh['side'=2,'col'=32,'hid'=4] {'side','hid'}, use_global_device_ids=true, to_apply=%region_6.7 | all-reduce | flops 2097152 | bytes 12582912 | tf_op jit(solution)/shard_map/psum | solution.py:62
  377.6 1.9 dynamic-slice_convert_fusion
  379.5 2.2 reshape.115
  381.7 8.4 %all-to-all-start.1 = ((bf16[32,2,4096]{2,1,0:T(2,128)(2,1)}), bf16[32,2,4096]{2,1,0:T(2,128)(2,1)}, u32[]{:S(2)}, u32[]{:S(2)}) async-start(bf16[32,2,4096]{2,1,0:T(2,128)(2,1)} %reshape.115), calls=%async_computation.1 | async-start | bytes 1048576 | tf_op jit(solution)/shard_map/all_to_all | solution.py:65
  390.1 0.6 mul.87
  390.7 0.8 copy.27
  391.5 0.7 fusion.19
  392.2 15.4 %all-to-all-done.1 = bf16[32,2,4096]{2,1,0:T(2,128)(2,1)} async-done(((bf16[32,2,4096]{2,1,0:T(2,128)(2,1)}), bf16[32,2,4096]{2,1,0:T(2,128)(2,1)}, u32[]{:S(2)}, u32[]{:S(2)}) %all-to-all-start.1) | async-done | bytes 524320 | tf_op jit(solution)/shard_map/all_to_all | solution.py:65
  407.6 2.0 reshape.116
  409.7 3.0 gather_fusion
  412.7 2.0 gather.7
  414.7 1.9 multiply_reduce_fusion
  416.6 0.8 add_convert_fusion
  (7 shorter events, 0.0 us)
Async XLA Ops:
  6.5 196.2 %copy-start = (bf16[1,384,4096]{2,1,0:T(8,128)(2,1)S(1)}, bf16[1,384,4096]{2,1,0:T(8,128)(2,1)}, u32[]{:S(2)}) copy-start(bf16[1,384,4096]{2,1,0:T(8,128)(2,1)} %param.17) | copy-start | bytes 9437188
  6.5 7.8 %copy-start.1 = (bf16[16,4096]{1,0:T(8,128)(2,1)S(1)}, bf16[16,4096]{1,0:T(8,128)(2,1)}, u32[]{:S(2)}) copy-start(bf16[16,4096]{1,0:T(8,128)(2,1)} %param.9) | copy-start | bytes 393220
  6.5 8.7 %copy-start.3 = (s32[16,3]{0,1:T(4,128)S(1)}, s32[16,3]{0,1:T(4,128)}, u32[]{:S(2)}) copy-start(s32[16,3]{0,1:T(4,128)} %param.13) | copy-start | bytes 580
  6.5 58.8 %all-gather.2.cloned.1.call-start = ((), (), s32[]{:S(2)}) async-start(), calls=%async_computation.2 | async-start | bytes 4718592 | tf_op jit(solution)/shard_map/all_gather | solution.py:52
  10.2 0.8 copy-start.2
  18.4 0.6 copy-start.4
  74.0 104.4 %all-to-all-start = ((bf16[8,32,2,4096]{3,2,0,1:T(2,128)(2,1)}), bf16[8,32,2,4096]{3,2,0,1:T(2,128)(2,1)}, u32[]{:S(2)}, u32[]{:S(2)}) async-start(bf16[8,32,2,4096]{3,2,0,1:T(2,128)(2,1)} %copy.32), calls=%async_computation | async-start | bytes 8388608 | tf_op jit(solution)/shard_map/all_to_all | solution.py:53
  381.7 26.0 %all-to-all-start.1 = ((bf16[32,2,4096]{2,1,0:T(2,128)(2,1)}), bf16[32,2,4096]{2,1,0:T(2,128)(2,1)}, u32[]{:S(2)}, u32[]{:S(2)}) async-start(bf16[32,2,4096]{2,1,0:T(2,128)(2,1)} %reshape.115), calls=%async_computation.1 | async-start | bytes 1048576 | tf_op jit(solution)/shard_map/all_to_all | solution.py:65
Sparse Core Ops, SparseCore 0:
  28.7 36.5 all-gather.1
where the time goes:
time: 426 us; the launch traced here: 424 us
  blocking collectives  169 us (40%)
  waiting for transfers between devices  140 us (33%)
  local copies, waits for them, and re-layouts  53.2 us (12%)
  matrix products  18.7 us (4%)
  starting transfers between devices  18.6 us (4%)
  between operations  13.5 us (3%)
  other arithmetic  11 us (3%)
    psum x1, blocking collectives, on_device(): summed = lax.psum(partial_out, ('side', 'hid'))  169 us
    all_to_all x1, waiting for transfers between devices, on_device(): lax.all_to_all(grouped, 'col', split_axis=1, concat_axis=1, tiled=True)  87.7 us
    all_gather x1, waiting for transfers between devices, on_device(): lax.all_gather(dispatch[None], ('side', 'hid'), axis=0, tiled=True)  36.7 us
    all_to_all x1, waiting for transfers between devices, on_device(): lax.all_to_all(expert_out, 'col', split_axis=0, concat_axis=0, tiled=True)  15.4 us
    all_to_all x1, starting transfers between devices, on_device(): lax.all_to_all(grouped, 'col', split_axis=1, concat_axis=1, tiled=True)  10.2 us
    all_to_all x1, local copies, waits for them, and re-layouts, on_device(): lax.all_to_all(grouped, 'col', split_axis=1, concat_axis=1, tiled=True)  10.1 us
    unnamed x14, local copies, waits for them, and re-layouts  9.83 us
    all_gather x1, local copies, waits for them, and re-layouts, on_device(): lax.all_gather(dispatch[None], ('side', 'hid'), axis=0, tiled=True)  8.64 us
  transfers between devices with their start and end apart: 3, of which 3 were waited for; matrix products, arithmetic and copies ran while one was open for 2% of the time, Pallas kernels for 0%

commit v1 on v0

v1 whole, which is shorter than its diff:
```python
import math

import jax
import jax.numpy as jnp
from jax import lax
from jax.experimental import pallas as pl
from jax.experimental.pallas import tpu as pltpu
from jax.sharding import PartitionSpec as P

HEADS = 32
HD = 128
COLS = 32
NY = 4
NZ = 8
NX = 4
GROUPS = 4
PER = 8
CHUNK = 512
DZ = (0, 1, -2, 3, -3, 4, -1, 2)
MESH = pl.DeviceIdType.MESH
F32 = jnp.float32
BF16 = jnp.bfloat16


def iota(shape, axis):
    return lax.broadcasted_iota(jnp.int32, shape, axis)


def kernel(
    q_ref, res_ref, kv_ref, len_ref, ids_ref, rw_ref, gain_ref, wgu_hbm, wd_hbm,
    out_ref,
    qf, sc, att, hid, ns, tmp_i, tmp_w, sel, wt_hi, wt_lo, acc,
    disp, arr, rsend, ret, x, pf, pown, r1, sa, ta, sb, fin,
    wraw, wgu, wd,
    w_sem, d_send, d_recv, g_send, g_recv, r_send, r_recv, e_send, e_recv,
):
    side = lax.axis_index("side")
    col = lax.axis_index("col")
    hidx = lax.axis_index("hid")
    zc = col // NY
    yc = lax.rem(col, NY)
    rows, width = res_ref.shape
    half = width // 2

    def column(i, sign):
        dz, dy = DZ[i // NY], i % NY
        return lax.rem(zc + (sign * dz + NZ), NZ) * NY + lax.rem(yc + (sign * dy + NY), NY)

    def on_col(i, sign):
        return {"side": side, "col": column(i, sign), "hid": hidx}

    up = {"side": side, "col": col, "hid": lax.rem(hidx + 1, NX)}
    down = {"side": side, "col": col, "hid": lax.rem(hidx + NX - 1, NX)}
    partner = {"side": 1 - side, "col": col, "hid": hidx}

    def remote(src, dst, send, recv, device):
        return pltpu.make_async_remote_copy(
            src_ref=src, dst_ref=dst, send_sem=send, recv_sem=recv,
            device_id=device, device_id_type=MESH,
        )

    barrier = pltpu.get_barrier_semaphore()
    for device in [on_col(i, 1) for i in range(1, COLS)] + [up, down, partner]:
        pl.semaphore_signal(barrier, inc=1, device_id=device, device_id_type=MESH)

    w_copies = [
        pltpu.make_async_copy(
            wgu_hbm.at[:, :, pl.ds(l * 128, 128)],
            wraw.at[l],
            w_sem.at[l],
        )
        for l in range(3)
    ] + [pltpu.make_async_copy(wd_hbm, wd, w_sem.at[3])]
    for copy in w_copies:
        copy.start()

    tmp_i[...] = jnp.zeros_like(tmp_i)
    tmp_w[...] = jnp.zeros_like(tmp_w)
    tmp_i[0:3, 0:rows] = ids_ref[...]
    tmp_w[0:3, 0:rows] = rw_ref[...]
    ids_all = tmp_i[...]
    w_all = tmp_w[...]
    for shift in (16, 32, 64):
        ids_all = ids_all + pltpu.roll(ids_all, shift, 1)
        w_all = w_all + pltpu.roll(w_all, shift, 1)
    square = (128, 128)
    lane, sub = iota(square, 1), iota(square, 0)
    earlier = jnp.where(
        ((sub >> 4) == (lane >> 4)) & ((sub & 15) < (lane & 15)), 1.0, 0.0
    ).astype(BF16)
    same_part = (sub & 7) == (lane >> 4)
    rank_want = ((sub >> 3) & 1).astype(F32)
    for g in range(GROUPS):
        dz = jnp.where((sub >> 6) == 0, DZ[2 * g], DZ[2 * g + 1])
        dy = (sub >> 4) & 3
        expert = ((zc + dz + NZ) & (NZ - 1)) * NY + ((yc + dy) & (NY - 1))
        named = jnp.zeros(square, F32)
        weight = jnp.zeros(square, F32)
        for k in range(3):
            hit = expert == ids_all[k : k + 1, :]
            named = named + jnp.where(hit, 1.0, 0.0)
            weight = weight + jnp.where(hit, w_all[k : k + 1, :], 0.0)
        rank = jnp.dot(named.astype(BF16), earlier, preferred_element_type=F32)
        here = (named > 0.5) & (jnp.abs(rank - rank_want) < 0.5) & same_part
        sel[g] = jnp.where(here, 1.0, 0.0).astype(BF16)
        weight_t = jnp.where(here, weight, 0.0).T
        high = weight_t.astype(BF16)
        wt_hi[g] = high
        wt_lo[g] = (weight_t - high.astype(F32)).astype(BF16)

    for head in range(HEADS):
        qf[pl.ds(head * rows, rows), :] = q_ref[:, pl.ds(head * HD, HD)].astype(F32)
    positions = iota((HEADS, kv_ref.shape[1]), 1)
    for r in range(rows):
        q_r = qf[pl.ds(r, HEADS, stride=rows), :].astype(BF16)
        s_r = lax.dot_general(
            q_r, kv_ref[r, :, 0:HD], (((1,), (1,)), ((), ())), preferred_element_type=F32
        ) * (1.0 / math.sqrt(HD))
        sc[pl.ds(r * HEADS, HEADS), :] = jnp.where(positions < len_ref[r], s_r, -1e30)
    for r in range(rows):
        s_r = sc[pl.ds(r * HEADS, HEADS), :]
        e_r = jnp.exp(s_r - jnp.max(s_r, axis=1, keepdims=True))
        p_r = (e_r / jnp.sum(e_r, axis=1, keepdims=True)).astype(BF16)
        att[pl.ds(r, HEADS, stride=rows), :] = jnp.dot(
            p_r, kv_ref[r, :, HD : 2 * HD], preferred_element_type=F32
        )
    total = jnp.zeros((rows, HD), F32)
    for head in range(HEADS):
        lanes = pl.ds(head * HD, HD)
        h_part = res_ref[:, lanes].astype(F32) + att[pl.ds(head * rows, rows), :]
        hid[:, lanes] = h_part
        total = total + h_part * h_part
    scale = lax.rsqrt(jnp.sum(total, axis=1, keepdims=True) * (1.0 / width) + 1e-6)
    for j in range(PER):
        lanes = pl.ds(j * CHUNK, CHUNK)
        ns[pl.ds(j * rows, rows), :] = (hid[:, lanes] * scale * gain_ref[:, lanes]).astype(BF16)

    def d_copy(i):
        return remote(disp.at[i], arr.at[i], d_send.at[i], d_recv.at[i], on_col(i, 1))

    pl.semaphore_wait(barrier, COLS - 1 + 3)
    for g in range(GROUPS):
        block = jnp.dot(sel[g], ns[...], preferred_element_type=F32).astype(BF16)
        for k in range(PER):
            i = g * PER + k
            piece = block[k * 16 : (k + 1) * 16, :]
            if i == 0:
                arr[0] = piece
            else:
                disp[i] = piece
        for i in range(max(1, g * PER), (g + 1) * PER):
            d_copy(i).start()

    to_rows = jnp.where(
        lane == ((sub & 15) >> 1) * 16 + (sub & 1) * 8 + (sub >> 4), 1.0, 0.0
    ).astype(BF16)
    to_blocks = jnp.where(
        lane == (sub & 7) * 16 + (sub >> 4) * 2 + ((sub >> 3) & 1), 1.0, 0.0
    ).astype(BF16)

    wide = (256, 256)
    apart = jnp.where(
        iota(wide, 1) == 2 * (iota(wide, 0) & 127) + (iota(wide, 0) >> 7), 1.0, 0.0
    ).astype(BF16)

    def take_apart(l):
        w_copies[l].wait()
        raw = wraw.at[l].reshape(8192, 128)

        def body(t, carry):
            start = pl.multiple_of(t * 256, 256)
            pair = jnp.dot(
                apart, raw[pl.ds(start, 256), :], preferred_element_type=F32
            ).astype(BF16)
            there = pl.ds(pl.multiple_of(t * 128, 128), 128)
            wgu[l, there, 0:128] = pair[0:128, :]
            wgu[l, there, 128:256] = pair[128:256, :]
            return carry

        lax.fori_loop(0, 32, body, 0, unroll=4)

    def g_copy(g, which):
        src, dst, device = {
            0: (x.at[g, 0, 0], x.at[g, 0, 1], up),
            1: (x.at[g, 0, 0], x.at[g, 0, 2], down),
            2: (x.at[g, 0, 1, :, pl.ds(0, half)], x.at[g, 0, 3, :, pl.ds(0, half)], up),
            3: (x.at[g, 0, 2, :, pl.ds(half, half)], x.at[g, 0, 3, :, pl.ds(half, half)], down),
            4: (x.at[g, 0, 0], x.at[g, 1, 0], partner),
            5: (x.at[g, 0, 1], x.at[g, 1, 1], partner),
            6: (x.at[g, 0, 2], x.at[g, 1, 2], partner),
            7: (x.at[g, 0, 3], x.at[g, 1, 3], partner),
        }[which]
        return remote(src, dst, g_send.at[g, which], g_recv.at[g, which], device)

    def gather_own(g):
        for i in range(max(1, g * PER), (g + 1) * PER):
            d_copy(i).wait_recv()
        blocks = arr[pl.ds(g * PER, PER)].reshape(128, CHUNK)
        rows_g = jnp.dot(to_rows, blocks, preferred_element_type=F32).astype(BF16)
        for j in range(PER):
            x[g, 0, 0, :, pl.ds(j * CHUNK, CHUNK)] = rows_g[j * 16 : (j + 1) * 16, :]
        for which in (0, 1, 4):
            g_copy(g, which).start()

    def gather_on(g):
        g_copy(g, 0).wait_recv()
        g_copy(g, 2).start()
        g_copy(g, 5).start()
        g_copy(g, 1).wait_recv()
        g_copy(g, 3).start()
        g_copy(g, 6).start()

    def gather_far(g):
        g_copy(g, 2).wait_recv()
        g_copy(g, 3).wait_recv()
        g_copy(g, 7).start()

    def r_copy(g, which):
        low, high = pl.ds(0, half), pl.ds(half, half)
        src, dst, device = {
            0: (pown.at[g], r1.at[g], partner),
            1: (sa.at[g, 0], ta.at[g, 0], up),
            2: (sa.at[g, 1], ta.at[g, 1], down),
            3: (sa.at[g, 2], fin.at[g, 0, :, high], up),
            4: (sa.at[g, 3], fin.at[g, 1, :, low], down),
            5: (sb.at[g, 0], fin.at[g, 0, :, low], up),
            6: (sb.at[g, 1], fin.at[g, 1, :, high], down),
        }[which]
        return remote(src, dst, r_send.at[g, which], r_recv.at[g, which], device)

    def experts(g):
        for which in (4, 5, 6, 7):
            g_copy(g, which).wait_recv()
        rows_g = x[g].reshape(128, width)
        parts = []
        for l in range(3):
            both = jnp.dot(rows_g, wgu[l], preferred_element_type=F32)
            gate, upper = both[:, 0:128], both[:, 128:256]
            parts.append((gate / (1.0 + jnp.exp(-gate)) * upper).astype(BF16))
        act = jnp.concatenate(parts, axis=1)
        for n in range(8):
            lanes = pl.ds(n * CHUNK, CHUNK)
            part = jnp.dot(act, wd[:, lanes], preferred_element_type=F32)
            pf[g, :, lanes] = part[0:64, :]
            for rel in range(4):
                pown[g, rel, :, lanes] = part[64 + rel * 16 : 80 + rel * 16, :].astype(BF16)
        r_copy(g, 0).start()

    def chip_sum(g):
        r_copy(g, 0).wait_recv()
        low, high = pl.ds(0, half), pl.ds(half, half)

        def both(rel, lanes):
            return pf[g, pl.ds(rel * 16, 16), lanes] + r1[g, rel, :, lanes].astype(F32)

        sa[g, 0] = both(3, low).astype(BF16)
        r_copy(g, 1).start()
        sa[g, 1] = both(3, high).astype(BF16)
        r_copy(g, 2).start()
        sa[g, 2] = both(2, high).astype(BF16)
        r_copy(g, 3).start()
        sa[g, 3] = both(1, low).astype(BF16)
        r_copy(g, 4).start()

    def pass_on(g):
        low, high = pl.ds(0, half), pl.ds(half, half)

        def both(rel, lanes):
            return pf[g, pl.ds(rel * 16, 16), lanes] + r1[g, rel, :, lanes].astype(F32)

        r_copy(g, 1).wait_recv()
        sb[g, 0] = (both(2, low) + ta[g, 0].astype(F32)).astype(BF16)
        r_copy(g, 5).start()
        r_copy(g, 2).wait_recv()
        sb[g, 1] = (both(1, high) + ta[g, 1].astype(F32)).astype(BF16)
        r_copy(g, 6).start()

    def e_copy(i):
        return remote(rsend.at[i], ret.at[i], e_send.at[i], e_recv.at[i], on_col(i, -1))

    def give_back(g):
        for which in (3, 4, 5, 6):
            r_copy(g, which).wait_recv()
        pieces = []
        for j in range(PER):
            lanes = pl.ds(j * CHUNK, CHUNK)
            whole = pf[g, 0:16, lanes] + r1[g, 0, :, lanes].astype(F32)
            whole = whole + fin[g, 0, :, lanes].astype(F32) + fin[g, 1, :, lanes].astype(F32)
            pieces.append(whole.astype(BF16))
        blocks = jnp.dot(
            to_blocks, jnp.concatenate(pieces, axis=0), preferred_element_type=F32
        ).astype(BF16)
        for k in range(PER):
            i = g * PER + k
            piece = blocks[k * 16 : (k + 1) * 16, :]
            if i == 0:
                ret[0] = piece
            else:
                rsend[i] = piece
        for i in range(max(1, g * PER), (g + 1) * PER):
            e_copy(i).start()

    def combine(g):
        for i in range(max(1, g * PER), (g + 1) * PER):
            e_copy(i).wait_recv()
        blocks = ret[pl.ds(g * PER, PER)].reshape(128, CHUNK)
        part = jnp.dot(wt_hi[g], blocks, preferred_element_type=F32) + jnp.dot(
            wt_lo[g], blocks, preferred_element_type=F32
        )
        if g == 0:
            acc[...] = part
        else:
            acc[...] = acc[...] + part

    take_apart(0)
    gather_own(0)
    take_apart(1)
    gather_own(1)
    take_apart(2)
    gather_on(0)
    gather_far(0)
    gather_on(1)
    gather_own(2)
    w_copies[3].wait()
    experts(0)
    gather_far(1)
    chip_sum(0)
    gather_on(2)
    gather_own(3)
    experts(1)
    pass_on(0)
    gather_far(2)
    chip_sum(1)
    gather_on(3)
    experts(2)
    give_back(0)
    pass_on(1)
    gather_far(3)
    chip_sum(2)
    experts(3)
    give_back(1)
    pass_on(2)
    chip_sum(3)
    combine(0)
    give_back(2)
    pass_on(3)
    combine(1)
    give_back(3)
    combine(2)
    combine(3)

    for j in range(PER):
        lanes = pl.ds(j * CHUNK, CHUNK)
        out_ref[:, lanes] = (hid[:, lanes] + acc[pl.ds(j * rows, rows), :]).astype(BF16)

    for i in range(1, COLS):
        d_copy(i).wait_send()
        e_copy(i).wait_send()
    for g in range(GROUPS):
        for which in range(8):
            g_copy(g, which).wait_send()
        for which in range(7):
            r_copy(g, which).wait_send()


def on_device(
    residual, queries, key_values, lengths, route_ids, route_weights, norm_gain, w_gate_up, w_down
):
    rows, width = residual.shape
    vmem = pl.BlockSpec(memory_space=pltpu.VMEM)
    anywhere = pl.BlockSpec(memory_space=pl.ANY)
    half = width // 2
    return pl.pallas_call(
        kernel,
        out_shape=jax.ShapeDtypeStruct((rows, width), BF16),
        in_specs=[
            vmem, vmem, vmem, pl.BlockSpec(memory_space=pltpu.SMEM), vmem, vmem, vmem,
            anywhere, anywhere,
        ],
        out_specs=vmem,
        scratch_shapes=[
            pltpu.VMEM((HEADS * rows, HD), F32),
            pltpu.VMEM((HEADS * rows, key_values.shape[1]), F32),
            pltpu.VMEM((HEADS * rows, HD), F32),
            pltpu.VMEM((rows, width), F32),
            pltpu.VMEM((PER * rows, CHUNK), BF16),
            pltpu.VMEM((8, 128), jnp.int32),
            pltpu.VMEM((8, 128), F32),
            pltpu.VMEM((GROUPS, 128, 128), BF16),
            pltpu.VMEM((GROUPS, 128, 128), BF16),
            pltpu.VMEM((GROUPS, 128, 128), BF16),
            pltpu.VMEM((PER * rows, CHUNK), F32),
            pltpu.VMEM((COLS, 16, CHUNK), BF16),
            pltpu.VMEM((COLS, 16, CHUNK), BF16),
            pltpu.VMEM((COLS, 16, CHUNK), BF16),
            pltpu.VMEM((COLS, 16, CHUNK), BF16),
            pltpu.VMEM((GROUPS, 2, 4, 16, width), BF16),
            pltpu.VMEM((GROUPS, 64, width), F32),
            pltpu.VMEM((GROUPS, 4, 16, width), BF16),
            pltpu.VMEM((GROUPS, 4, 16, width), BF16),
            pltpu.VMEM((GROUPS, 4, 16, half), BF16),
            pltpu.VMEM((GROUPS, 2, 16, half), BF16),
            pltpu.VMEM((GROUPS, 2, 16, half), BF16),
            pltpu.VMEM((GROUPS, 2, 16, width), BF16),
            pltpu.VMEM((3, 4096, 2, 128), BF16),
            pltpu.VMEM((3, 4096, 256), BF16),
            pltpu.VMEM((384, 4096), BF16),
            pltpu.SemaphoreType.DMA((4,)),
            pltpu.SemaphoreType.DMA((COLS,)),
            pltpu.SemaphoreType.DMA((COLS,)),
            pltpu.SemaphoreType.DMA((GROUPS, 8)),
            pltpu.SemaphoreType.DMA((GROUPS, 8)),
            pltpu.SemaphoreType.DMA((GROUPS, 7)),
            pltpu.SemaphoreType.DMA((GROUPS, 7)),
            pltpu.SemaphoreType.DMA((COLS,)),
            pltpu.SemaphoreType.DMA((COLS,)),
        ],
        compiler_params=pltpu.CompilerParams(
            collective_id=0, has_side_effects=True, vmem_limit_bytes=60 * 2**20
        ),
        name="moe_step",
    )(
        queries, residual, key_values, lengths, route_ids.T, route_weights.T,
        norm_gain.reshape(1, width), w_gate_up[0], w_down[0],
    )


def solution(mesh):
    placed = (
        P(("side", "col", "hid"), None),
        P(("side", "col", "hid"), None),
        P(("side", "col", "hid"), None, None),
        P(("side", "col", "hid")),
        P(("side", "col", "hid"), None),
        P(("side", "col", "hid"), None),
        P(),
        P("col", None, None, ("side", "hid")),
        P("col", ("side", "hid"), None),
    )
    return jax.shard_map(
        on_device,
        mesh=mesh,
        in_specs=placed,
        out_specs=P(("side", "col", "hid"), None),
        check_vma=False,
    )
```

time: 426 us -> 76.4 us (0.18)
  the two profiles are of different devices: /device:TPU:2 before, /device:TPU:1 now
where the time goes in v1:
time: 76.4 us; the launch traced here: 76.3 us
  Pallas kernels  74.7 us (98%)
  local copies, waits for them, and re-layouts  1.57 us (2%)
    pallas_call x1, Pallas kernels, on_device(): pl.pallas_call(kernel, out_shape=jax.ShapeDtypeStruct((rows, width), BF16...  74.7 us
    unnamed x1, local copies, waits for them, and re-layouts  1.57 us

profile of v1, /device:TPU:1, one launch (start us, length us, event | category | flops | bytes accessed | tf_op | source)
XLA Modules:
  0.0 76.3 jit_solution(17803742201475770964)
XLA Ops:
  0.0 74.7 %moe_step.1 = bf16[16,4096]{1,0:T(8,128)(2,1)} custom-call(bf16[16,4096]{1,0:T(8,128)(2,1)} %q_ref.1, bf16[16,4096]{1,0:T(8,128)(2,1)} %res_ref.1, bf16[16,256,256]{2,1,0:T(8,128)(2,1)} %kv_ref.1, s32[16]{0:T(128)} %len_ref.1, s32[3,16]{1,0:T(4,128)} %bitcast.8, f32[3,16]{1,0:T(4,128)} %bitcast.9, f32[1,4096]{1,0:T(1,128)} %bitcast.7, ...), custom_call_target="tpu_custom_call" | custom-call | tf_op jit(solution)/shard_map/moe_step/pallas_call | solution.py:373
  74.7 1.6 %copy.11 = bf16[16,4096]{1,0:T(8,128)(2,1)} copy(bf16[16,4096]{1,0:T(8,128)(2,1)} %moe_step.1) | data formatting | bytes 262144

commit v2 on v1

--- a/solution.py
+++ b/solution.py
@@ -17,6 +17,16 @@
 PER = 8
 CHUNK = 512
 DZ = (0, 1, -2, 3, -3, 4, -1, 2)
+SCHEDULE = (
+    ("apart", 0), ("apart", 1), ("apart", 2), ("apart", 3), ("own", 0),
+    ("down", 0), ("up", 0), ("own", 1), ("own", 2), ("up", 1),
+    ("down", 1), ("own", 3), ("up", 2), ("down", 2), ("experts", 1),
+    ("down", 3), ("up", 3), ("experts", 2), ("pass_down", 1), ("pass_up", 1),
+    ("experts", 0), ("pass_up", 2), ("pass_down", 2), ("back", 1), ("experts", 3),
+    ("back", 2), ("pass_up", 0), ("pass_down", 0), ("pass_up", 3), ("pass_down", 3),
+    ("back", 0), ("back", 3), ("combine", 0), ("combine", 1), ("combine", 2),
+    ("combine", 3),
+)
 MESH = pl.DeviceIdType.MESH
 F32 = jnp.float32
 BF16 = jnp.bfloat16
@@ -30,9 +40,9 @@
     q_ref, res_ref, kv_ref, len_ref, ids_ref, rw_ref, gain_ref, wgu_hbm, wd_hbm,
     out_ref,
     qf, sc, att, hid, ns, tmp_i, tmp_w, sel, wt_hi, wt_lo, acc,
-    disp, arr, rsend, ret, x, pf, pown, r1, sa, ta, sb, fin,
+    disp, arr, rsend, ret, x, pf, sa, ta, sb, fin,
     wraw, wgu, wd,
-    w_sem, d_send, d_recv, g_send, g_recv, r_send, r_recv, e_send, e_recv,
+    w_sem, p_send, p_recv, d_send, d_recv, g_send, g_recv, r_send, r_recv, e_send, e_recv,
 ):
     side = lax.axis_index("side")
     col = lax.axis_index("col")
@@ -59,6 +69,16 @@
             device_id=device, device_id_type=MESH,
         )
 
+    begun, landed = [], set()
+
+    def start(make, *key):
+        make(*key).start()
+        begun.append((make, key))
+
+    def arrive(make, *key):
+        make(*key).wait_recv()
+        landed.add((make, key))
+
     barrier = pltpu.get_barrier_semaphore()
     for device in [on_col(i, 1) for i in range(1, COLS)] + [up, down, partner]:
         pl.semaphore_signal(barrier, inc=1, device_id=device, device_id_type=MESH)
@@ -70,7 +90,7 @@
             w_sem.at[l],
         )
         for l in range(3)
-    ] + [pltpu.make_async_copy(wd_hbm, wd, w_sem.at[3])]
+    ] + [pltpu.make_async_copy(wd_hbm, wd.at[pl.ds(0, 384)], w_sem.at[3])]
     for copy in w_copies:
         copy.start()
 
@@ -149,7 +169,7 @@
             else:
                 disp[i] = piece
         for i in range(max(1, g * PER), (g + 1) * PER):
-            d_copy(i).start()
+            start(d_copy, i)
 
     to_rows = jnp.where(
         lane == ((sub & 15) >> 1) * 16 + (sub & 1) * 8 + (sub >> 4), 1.0, 0.0
@@ -163,129 +183,136 @@
         iota(wide, 1) == 2 * (iota(wide, 0) & 127) + (iota(wide, 0) >> 7), 1.0, 0.0
     ).astype(BF16)
 
-    def take_apart(l):
-        w_copies[l].wait()
-        raw = wraw.at[l].reshape(8192, 128)
+    def p_copy(which):
+        if which == 4:
+            src, dst = wd.at[pl.ds(0, 384)], wd.at[pl.ds(384, 384)]
+        else:
+            deep = pl.ds(which * 1024, 1024)
+            src, dst = wgu.at[0, :, deep, :], wgu.at[1, :, deep, :]
+        return remote(src, dst, p_send.at[which], p_recv.at[which], partner)
+
+    def take_apart(part):
+        if part == 0:
+            w_copies[3].wait()
+            start(p_copy, 4)
+            for l in range(3):
+                w_copies[l].wait()
+        raws = [wraw.at[l].reshape(8192, 128) for l in range(3)]
 
         def body(t, carry):
-            start = pl.multiple_of(t * 256, 256)
-            pair = jnp.dot(
-                apart, raw[pl.ds(start, 256), :], preferred_element_type=F32
-            ).astype(BF16)
-            there = pl.ds(pl.multiple_of(t * 128, 128), 128)
-            wgu[l, there, 0:128] = pair[0:128, :]
-            wgu[l, there, 128:256] = pair[128:256, :]
+            first = part * 2048 + t * 512
+            both = jnp.concatenate(
+                [raw[pl.ds(pl.multiple_of(first + d, 256), 256), :] for d in (0, 256) for raw in raws],
+                axis=1,
+            )
+            pair = jnp.dot(apart, both, preferred_element_type=F32).astype(BF16)
+            for d in range(2):
+                there = pl.ds(pl.multiple_of(part * 1024 + t * 256 + d * 128, 128), 128)
+                for l in range(3):
+                    lanes = slice((d * 3 + l) * 128, (d * 3 + l + 1) * 128)
+                    wgu[0, l, there, 0:128] = pair[0:128, lanes]
+                    wgu[0, l, there, 128:256] = pair[128:256, lanes]
             return carry
 
-        lax.fori_loop(0, 32, body, 0, unroll=4)
+        lax.fori_loop(0, 4, body, 0, unroll=2)
+        start(p_copy, part)
+
+    low, high = pl.ds(0, half), pl.ds(half, half)
 
     def g_copy(g, which):
         src, dst, device = {
-            0: (x.at[g, 0, 0], x.at[g, 0, 1], up),
-            1: (x.at[g, 0, 0], x.at[g, 0, 2], down),
-            2: (x.at[g, 0, 1, :, pl.ds(0, half)], x.at[g, 0, 3, :, pl.ds(0, half)], up),
-            3: (x.at[g, 0, 2, :, pl.ds(half, half)], x.at[g, 0, 3, :, pl.ds(half, half)], down),
-            4: (x.at[g, 0, 0], x.at[g, 1, 0], partner),
-            5: (x.at[g, 0, 1], x.at[g, 1, 1], partner),
-            6: (x.at[g, 0, 2], x.at[g, 1, 2], partner),
-            7: (x.at[g, 0, 3], x.at[g, 1, 3], partner),
+            0: (x.at[g, 0, :, low], x.at[g, 1, :, low], up),
+            1: (x.at[g, 0, :, high], x.at[g, 1, :, high], up),
+            2: (x.at[g, 0, :, high], x.at[g, 2, :, high], down),
+            3: (x.at[g, 0, :, low], x.at[g, 2, :, low], down),
+            4: (x.at[g, 1, :, low], x.at[g, 3, :, low], up),
+            5: (x.at[g, 2, :, high], x.at[g, 3, :, high], down),
         }[which]
         return remote(src, dst, g_send.at[g, which], g_recv.at[g, which], device)
 
     def gather_own(g):
         for i in range(max(1, g * PER), (g + 1) * PER):
-            d_copy(i).wait_recv()
+            arrive(d_copy, i)
         blocks = arr[pl.ds(g * PER, PER)].reshape(128, CHUNK)
         rows_g = jnp.dot(to_rows, blocks, preferred_element_type=F32).astype(BF16)
         for j in range(PER):
-            x[g, 0, 0, :, pl.ds(j * CHUNK, CHUNK)] = rows_g[j * 16 : (j + 1) * 16, :]
-        for which in (0, 1, 4):
-            g_copy(g, which).start()
-
-    def gather_on(g):
-        g_copy(g, 0).wait_recv()
-        g_copy(g, 2).start()
-        g_copy(g, 5).start()
-        g_copy(g, 1).wait_recv()
-        g_copy(g, 3).start()
-        g_copy(g, 6).start()
-
-    def gather_far(g):
-        g_copy(g, 2).wait_recv()
-        g_copy(g, 3).wait_recv()
-        g_copy(g, 7).start()
+            x[g, 0, :, pl.ds(j * CHUNK, CHUNK)] = rows_g[j * 16 : (j + 1) * 16, :]
+        for which in (0, 2, 1, 3):
+            start(g_copy, g, which)
+
+    def on_up(g):
+        arrive(g_copy, g, 0)
+        start(g_copy, g, 4)
+
+    def on_down(g):
+        arrive(g_copy, g, 2)
+        start(g_copy, g, 5)
 
     def r_copy(g, which):
-        low, high = pl.ds(0, half), pl.ds(half, half)
         src, dst, device = {
-            0: (pown.at[g], r1.at[g], partner),
-            1: (sa.at[g, 0], ta.at[g, 0], up),
-            2: (sa.at[g, 1], ta.at[g, 1], down),
-            3: (sa.at[g, 2], fin.at[g, 0, :, high], up),
-            4: (sa.at[g, 3], fin.at[g, 1, :, low], down),
-            5: (sb.at[g, 0], fin.at[g, 0, :, low], up),
-            6: (sb.at[g, 1], fin.at[g, 1, :, high], down),
+            0: (sa.at[g, 0], ta.at[g, 0], up),
+            1: (sa.at[g, 1], ta.at[g, 1], down),
+            2: (sa.at[g, 2], fin.at[g, 0, :, high], up),
+            3: (sa.at[g, 3], fin.at[g, 1, :, low], down),
+            4: (sb.at[g, 0], fin.at[g, 0, :, low], up),
+            5: (sb.at[g, 1], fin.at[g, 1, :, high], down),
         }[which]
         return remote(src, dst, r_send.at[g, which], r_recv.at[g, which], device)
 
     def experts(g):
-        for which in (4, 5, 6, 7):
-            g_copy(g, which).wait_recv()
-        rows_g = x[g].reshape(128, width)
+        if not ready:
+            for which in range(5):
+                arrive(p_copy, which)
+            ready.append(True)
+        for which in (1, 3, 4, 5):
+            arrive(g_copy, g, which)
+        rows_g = x[g].reshape(64, width)
         parts = []
-        for l in range(3):
-            both = jnp.dot(rows_g, wgu[l], preferred_element_type=F32)
-            gate, upper = both[:, 0:128], both[:, 128:256]
-            parts.append((gate / (1.0 + jnp.exp(-gate)) * upper).astype(BF16))
+        for core in range(2):
+            for l in range(3):
+                both = jnp.dot(rows_g, wgu[core, l], preferred_element_type=F32)
+                gate, upper = both[:, 0:128], both[:, 128:256]
+                parts.append((gate / (1.0 + jnp.exp(-gate)) * upper).astype(BF16))
         act = jnp.concatenate(parts, axis=1)
         for n in range(8):
             lanes = pl.ds(n * CHUNK, CHUNK)
+            there = pl.ds(n % 4 * CHUNK, CHUNK)
             part = jnp.dot(act, wd[:, lanes], preferred_element_type=F32)
-            pf[g, :, lanes] = part[0:64, :]
-            for rel in range(4):
-                pown[g, rel, :, lanes] = part[64 + rel * 16 : 80 + rel * 16, :].astype(BF16)
-        r_copy(g, 0).start()
-
-    def chip_sum(g):
-        r_copy(g, 0).wait_recv()
-        low, high = pl.ds(0, half), pl.ds(half, half)
-
-        def both(rel, lanes):
-            return pf[g, pl.ds(rel * 16, 16), lanes] + r1[g, rel, :, lanes].astype(F32)
-
-        sa[g, 0] = both(3, low).astype(BF16)
-        r_copy(g, 1).start()
-        sa[g, 1] = both(3, high).astype(BF16)
-        r_copy(g, 2).start()
-        sa[g, 2] = both(2, high).astype(BF16)
-        r_copy(g, 3).start()
-        sa[g, 3] = both(1, low).astype(BF16)
-        r_copy(g, 4).start()
-
-    def pass_on(g):
-        low, high = pl.ds(0, half), pl.ds(half, half)
-
-        def both(rel, lanes):
-            return pf[g, pl.ds(rel * 16, 16), lanes] + r1[g, rel, :, lanes].astype(F32)
-
-        r_copy(g, 1).wait_recv()
-        sb[g, 0] = (both(2, low) + ta[g, 0].astype(F32)).astype(BF16)
-        r_copy(g, 5).start()
-        r_copy(g, 2).wait_recv()
-        sb[g, 1] = (both(1, high) + ta[g, 1].astype(F32)).astype(BF16)
-        r_copy(g, 6).start()
+            pf[g, 0:16, lanes] = part[0:16, :]
+            if n < 4:
+                sa[g, 0, :, there] = part[48:64, :].astype(BF16)
+                sa[g, 3, :, there] = part[16:32, :].astype(BF16)
+                pf[g, 32:48, lanes] = part[32:48, :]
+            else:
+                sa[g, 1, :, there] = part[48:64, :].astype(BF16)
+                sa[g, 2, :, there] = part[32:48, :].astype(BF16)
+                pf[g, 16:32, lanes] = part[16:32, :]
+            if n == 3:
+                start(r_copy, g, 0)
+                start(r_copy, g, 3)
+        start(r_copy, g, 1)
+        start(r_copy, g, 2)
+
+    def pass_up(g):
+        arrive(r_copy, g, 0)
+        sb[g, 0] = (pf[g, 32:48, low] + ta[g, 0].astype(F32)).astype(BF16)
+        start(r_copy, g, 4)
+
+    def pass_down(g):
+        arrive(r_copy, g, 1)
+        sb[g, 1] = (pf[g, 16:32, high] + ta[g, 1].astype(F32)).astype(BF16)
+        start(r_copy, g, 5)
 
     def e_copy(i):
         return remote(rsend.at[i], ret.at[i], e_send.at[i], e_recv.at[i], on_col(i, -1))
 
     def give_back(g):
-        for which in (3, 4, 5, 6):
-            r_copy(g, which).wait_recv()
+        for which in (2, 3, 4, 5):
+            arrive(r_copy, g, which)
         pieces = []
         for j in range(PER):
             lanes = pl.ds(j * CHUNK, CHUNK)
-            whole = pf[g, 0:16, lanes] + r1[g, 0, :, lanes].astype(F32)
-            whole = whole + fin[g, 0, :, lanes].astype(F32) + fin[g, 1, :, lanes].astype(F32)
+            whole = pf[g, 0:16, lanes] + fin[g, 0, :, lanes].astype(F32) + fin[g, 1, :, lanes].astype(F32)
             pieces.append(whole.astype(BF16))
         blocks = jnp.dot(
             to_blocks, jnp.concatenate(pieces, axis=0), preferred_element_type=F32
@@ -298,69 +325,36 @@
             else:
                 rsend[i] = piece
         for i in range(max(1, g * PER), (g + 1) * PER):
-            e_copy(i).start()
+            start(e_copy, i)
 
     def combine(g):
         for i in range(max(1, g * PER), (g + 1) * PER):
-            e_copy(i).wait_recv()
+            arrive(e_copy, i)
         blocks = ret[pl.ds(g * PER, PER)].reshape(128, CHUNK)
         part = jnp.dot(wt_hi[g], blocks, preferred_element_type=F32) + jnp.dot(
             wt_lo[g], blocks, preferred_element_type=F32
         )
-        if g == 0:
+        if not summed:
+            summed.append(True)
             acc[...] = part
         else:
             acc[...] = acc[...] + part
 
-    take_apart(0)
-    gather_own(0)
-    take_apart(1)
-    gather_own(1)
-    take_apart(2)
-    gather_on(0)
-    gather_far(0)
-    gather_on(1)
-    gather_own(2)
-    w_copies[3].wait()
-    experts(0)
-    gather_far(1)
-    chip_sum(0)
-    gather_on(2)
-    gather_own(3)
-    experts(1)
-    pass_on(0)
-    gather_far(2)
-    chip_sum(1)
-    gather_on(3)
-    experts(2)
-    give_back(0)
-    pass_on(1)
-    gather_far(3)
-    chip_sum(2)
-    experts(3)
-    give_back(1)
-    pass_on(2)
-    chip_sum(3)
-    combine(0)
-    give_back(2)
-    pass_on(3)
-    combine(1)
-    give_back(3)
-    combine(2)
-    combine(3)
+    steps = {
+        "apart": take_apart, "own": gather_own, "up": on_up, "down": on_down,
+        "experts": experts, "pass_up": pass_up, "pass_down": pass_down, "back": give_back,
+        "combine": combine,
+    }
+    ready, summed = [], []
+    for name, number in SCHEDULE:
+        steps[name](number)
 
     for j in range(PER):
         lanes = pl.ds(j * CHUNK, CHUNK)
         out_ref[:, lanes] = (hid[:, lanes] + acc[pl.ds(j * rows, rows), :]).astype(BF16)
 
-    for i in range(1, COLS):
-        d_copy(i).wait_send()
-        e_copy(i).wait_send()
-    for g in range(GROUPS):
-        for which in range(8):
-            g_copy(g, which).wait_send()
-        for which in range(7):
-            r_copy(g, which).wait_send()
+    for make, key in begun:
+        make(*key).wait_send()
 
 
 def on_device(
@@ -394,24 +388,24 @@
             pltpu.VMEM((COLS, 16, CHUNK), BF16),
             pltpu.VMEM((COLS, 16, CHUNK), BF16),
             pltpu.VMEM((COLS, 16, CHUNK), BF16),
-            pltpu.VMEM((GROUPS, 2, 4, 16, width), BF16),
-            pltpu.VMEM((GROUPS, 64, width), F32),
             pltpu.VMEM((GROUPS, 4, 16, width), BF16),
-            pltpu.VMEM((GROUPS, 4, 16, width), BF16),
+            pltpu.VMEM((GROUPS, 48, width), F32),
             pltpu.VMEM((GROUPS, 4, 16, half), BF16),
             pltpu.VMEM((GROUPS, 2, 16, half), BF16),
             pltpu.VMEM((GROUPS, 2, 16, half), BF16),
             pltpu.VMEM((GROUPS, 2, 16, width), BF16),
             pltpu.VMEM((3, 4096, 2, 128), BF16),
-            pltpu.VMEM((3, 4096, 256), BF16),
-            pltpu.VMEM((384, 4096), BF16),
+            pltpu.VMEM((2, 3, 4096, 256), BF16),
+            pltpu.VMEM((768, 4096), BF16),
             pltpu.SemaphoreType.DMA((4,)),
+            pltpu.SemaphoreType.DMA((5,)),
+            pltpu.SemaphoreType.DMA((5,)),
             pltpu.SemaphoreType.DMA((COLS,)),
             pltpu.SemaphoreType.DMA((COLS,)),
-            pltpu.SemaphoreType.DMA((GROUPS, 8)),
-            pltpu.SemaphoreType.DMA((GROUPS, 8)),
-            pltpu.SemaphoreType.DMA((GROUPS, 7)),
-            pltpu.SemaphoreType.DMA((GROUPS, 7)),
+            pltpu.SemaphoreType.DMA((GROUPS, 6)),
+            pltpu.SemaphoreType.DMA((GROUPS, 6)),
+            pltpu.SemaphoreType.DMA((GROUPS, 6)),
+            pltpu.SemaphoreType.DMA((GROUPS, 6)),
             pltpu.SemaphoreType.DMA((COLS,)),
             pltpu.SemaphoreType.DMA((COLS,)),
         ],

time: 76.4 us -> 69.7 us (0.912)
  the two profiles are of different devices: /device:TPU:1 before, /device:TPU:2 now
where the time goes in v2:
time: 69.7 us; the launch traced here: 69.6 us
  Pallas kernels  68 us (98%)
  local copies, waits for them, and re-layouts  1.57 us (2%)
    pallas_call x1, Pallas kernels, on_device(): pl.pallas_call(kernel, out_shape=jax.ShapeDtypeStruct((rows, width), BF16...  68 us
    unnamed x1, local copies, waits for them, and re-layouts  1.57 us

profile of v2, /device:TPU:2, one launch (start us, length us, event | category | flops | bytes accessed | tf_op | source)
XLA Modules:
  0.0 69.6 jit_solution(2279486804643481716)
XLA Ops:
  0.0 68.0 %moe_step.1 = bf16[16,4096]{1,0:T(8,128)(2,1)} custom-call(bf16[16,4096]{1,0:T(8,128)(2,1)} %q_ref.1, bf16[16,4096]{1,0:T(8,128)(2,1)} %res_ref.1, bf16[16,256,256]{2,1,0:T(8,128)(2,1)} %kv_ref.1, s32[16]{0:T(128)} %len_ref.1, s32[3,16]{1,0:T(4,128)} %bitcast.8, f32[3,16]{1,0:T(4,128)} %bitcast.9, f32[1,4096]{1,0:T(1,128)} %bitcast.7, ...), custom_call_target="tpu_custom_call" | custom-call | tf_op jit(solution)/shard_map/moe_step/pallas_call | solution.py:367
  68.0 1.6 %copy.11 = bf16[16,4096]{1,0:T(8,128)(2,1)} copy(bf16[16,4096]{1,0:T(8,128)(2,1)} %moe_step.1) | data formatting | bytes 262144

commit v3 on v2

--- a/solution.py
+++ b/solution.py
@@ -18,15 +18,17 @@
 CHUNK = 512
 DZ = (0, 1, -2, 3, -3, 4, -1, 2)
 SCHEDULE = (
-    ("apart", 0), ("apart", 1), ("apart", 2), ("apart", 3), ("own", 0),
-    ("down", 0), ("up", 0), ("own", 1), ("own", 2), ("up", 1),
-    ("down", 1), ("own", 3), ("up", 2), ("down", 2), ("experts", 1),
-    ("down", 3), ("up", 3), ("experts", 2), ("pass_down", 1), ("pass_up", 1),
-    ("experts", 0), ("pass_up", 2), ("pass_down", 2), ("back", 1), ("experts", 3),
-    ("back", 2), ("pass_up", 0), ("pass_down", 0), ("pass_up", 3), ("pass_down", 3),
-    ("back", 0), ("back", 3), ("combine", 0), ("combine", 1), ("combine", 2),
-    ("combine", 3),
+    ("apart", 0), ("send", 2), ("apart", 1), ("send", 3), ("own", 0),
+    ("apart", 2), ("apart", 3), ("down", 0), ("up", 0), ("weigh", 0),
+    ("weigh", 1), ("weigh", 2), ("weigh", 3), ("own", 1), ("own", 2),
+    ("up", 1), ("down", 1), ("own", 3), ("up", 2), ("down", 2),
+    ("experts", 1), ("down", 3), ("up", 3), ("experts", 2), ("pass_down", 1),
+    ("pass_up", 1), ("experts", 0), ("pass_up", 2), ("pass_down", 2), ("back", 1),
+    ("experts", 3), ("back", 2), ("pass_up", 0), ("pass_down", 0), ("pass_up", 3),
+    ("pass_down", 3), ("back", 0), ("back", 3), ("combine", 0), ("combine", 1),
+    ("combine", 2), ("combine", 3),
 )
+EARLY = (0, 1)
 MESH = pl.DeviceIdType.MESH
 F32 = jnp.float32
 BF16 = jnp.bfloat16
@@ -37,12 +39,12 @@
 
 
 def kernel(
-    q_ref, res_ref, kv_ref, len_ref, ids_ref, rw_ref, gain_ref, wgu_hbm, wd_hbm,
+    q_ref, res_ref, kv_hbm, len_ref, ids_ref, rw_ref, gain_ref, wgu_hbm, wd_hbm,
     out_ref,
     qf, sc, att, hid, ns, tmp_i, tmp_w, sel, wt_hi, wt_lo, acc,
     disp, arr, rsend, ret, x, pf, sa, ta, sb, fin,
-    wraw, wgu, wd,
-    w_sem, p_send, p_recv, d_send, d_recv, g_send, g_recv, r_send, r_recv, e_send, e_recv,
+    wraw, wgu, wd, kv_ref,
+    kv_sem, w_sem, p_send, p_recv, d_send, d_recv, g_send, g_recv, r_send, r_recv, e_send, e_recv,
 ):
     side = lax.axis_index("side")
     col = lax.axis_index("col")
@@ -78,6 +80,9 @@
     def arrive(make, *key):
         make(*key).wait_recv()
         landed.add((make, key))
+
+    kv_copy = pltpu.make_async_copy(kv_hbm, kv_ref, kv_sem)
+    kv_copy.start()
 
     barrier = pltpu.get_barrier_semaphore()
     for device in [on_col(i, 1) for i in range(1, COLS)] + [up, down, partner]:
@@ -110,26 +115,33 @@
     ).astype(BF16)
     same_part = (sub & 7) == (lane >> 4)
     rank_want = ((sub >> 3) & 1).astype(F32)
-    for g in range(GROUPS):
+    def expert_of(g):
         dz = jnp.where((sub >> 6) == 0, DZ[2 * g], DZ[2 * g + 1])
         dy = (sub >> 4) & 3
-        expert = ((zc + dz + NZ) & (NZ - 1)) * NY + ((yc + dy) & (NY - 1))
+        return ((zc + dz + NZ) & (NZ - 1)) * NY + ((yc + dy) & (NY - 1))
+
+    for g in range(GROUPS):
+        expert = expert_of(g)
         named = jnp.zeros(square, F32)
-        weight = jnp.zeros(square, F32)
         for k in range(3):
-            hit = expert == ids_all[k : k + 1, :]
-            named = named + jnp.where(hit, 1.0, 0.0)
-            weight = weight + jnp.where(hit, w_all[k : k + 1, :], 0.0)
+            named = named + jnp.where(expert == ids_all[k : k + 1, :], 1.0, 0.0)
         rank = jnp.dot(named.astype(BF16), earlier, preferred_element_type=F32)
         here = (named > 0.5) & (jnp.abs(rank - rank_want) < 0.5) & same_part
         sel[g] = jnp.where(here, 1.0, 0.0).astype(BF16)
-        weight_t = jnp.where(here, weight, 0.0).T
-        high = weight_t.astype(BF16)
-        wt_hi[g] = high
-        wt_lo[g] = (weight_t - high.astype(F32)).astype(BF16)
+
+    def weigh(g):
+        expert = expert_of(g)
+        weight = jnp.zeros(square, F32)
+        for k in range(3):
+            weight = weight + jnp.where(expert == ids_all[k : k + 1, :], w_all[k : k + 1, :], 0.0)
+        weight_t = (weight * sel[g].astype(F32)).T
+        top_part = weight_t.astype(BF16)
+        wt_hi[g] = top_part
+        wt_lo[g] = (weight_t - top_part.astype(F32)).astype(BF16)
 
     for head in range(HEADS):
         qf[pl.ds(head * rows, rows), :] = q_ref[:, pl.ds(head * HD, HD)].astype(F32)
+    kv_copy.wait()
     positions = iota((HEADS, kv_ref.shape[1]), 1)
     for r in range(rows):
         q_r = qf[pl.ds(r, HEADS, stride=rows), :].astype(BF16)
@@ -158,6 +170,10 @@
     def d_copy(i):
         return remote(disp.at[i], arr.at[i], d_send.at[i], d_recv.at[i], on_col(i, 1))
 
+    def send(g):
+        for i in range(max(1, g * PER), (g + 1) * PER):
+            start(d_copy, i)
+
     pl.semaphore_wait(barrier, COLS - 1 + 3)
     for g in range(GROUPS):
         block = jnp.dot(sel[g], ns[...], preferred_element_type=F32).astype(BF16)
@@ -168,8 +184,8 @@
                 arr[0] = piece
             else:
                 disp[i] = piece
-        for i in range(max(1, g * PER), (g + 1) * PER):
-            start(d_copy, i)
+        if g in EARLY:
+            send(g)
 
     to_rows = jnp.where(
         lane == ((sub & 15) >> 1) * 16 + (sub & 1) * 8 + (sub >> 4), 1.0, 0.0
@@ -341,7 +357,7 @@
             acc[...] = acc[...] + part
 
     steps = {
-        "apart": take_apart, "own": gather_own, "up": on_up, "down": on_down,
+        "send": send, "weigh": weigh, "apart": take_apart, "own": gather_own, "up": on_up, "down": on_down,
         "experts": experts, "pass_up": pass_up, "pass_down": pass_down, "back": give_back,
         "combine": combine,
     }
@@ -368,7 +384,7 @@
         kernel,
         out_shape=jax.ShapeDtypeStruct((rows, width), BF16),
         in_specs=[
-            vmem, vmem, vmem, pl.BlockSpec(memory_space=pltpu.SMEM), vmem, vmem, vmem,
+            vmem, vmem, anywhere, pl.BlockSpec(memory_space=pltpu.SMEM), vmem, vmem, vmem,
             anywhere, anywhere,
         ],
         out_specs=vmem,
@@ -397,6 +413,8 @@
             pltpu.VMEM((3, 4096, 2, 128), BF16),
             pltpu.VMEM((2, 3, 4096, 256), BF16),
             pltpu.VMEM((768, 4096), BF16),
+            pltpu.VMEM(key_values.shape, BF16),
+            pltpu.SemaphoreType.DMA,
             pltpu.SemaphoreType.DMA((4,)),
             pltpu.SemaphoreType.DMA((5,)),
             pltpu.SemaphoreType.DMA((5,)),

time: 69.7 us -> 68.2 us (0.978)
  Pallas kernels: 68 us -> 66.5 us
    pallas_call x1, Pallas kernels: 68 us -> 66.5 us  [on_device(): pl.pallas_call(kernel, out_shape=jax.ShapeDtypeStruct((rows, width), BF16...]
where the time goes in v3:
time: 68.2 us; the launch traced here: 68.1 us
  Pallas kernels  66.5 us (98%)
  local copies, waits for them, and re-layouts  1.57 us (2%)
    pallas_call x1, Pallas kernels, on_device(): pl.pallas_call(kernel, out_shape=jax.ShapeDtypeStruct((rows, width), BF16...  66.5 us
    unnamed x1, local copies, waits for them, and re-layouts  1.57 us

profile of v3, /device:TPU:2, one launch (start us, length us, event | category | flops | bytes accessed | tf_op | source)
XLA Modules:
  0.0 68.1 jit_solution(12704545121575981266)
XLA Ops:
  0.0 66.5 %moe_step.1 = bf16[16,4096]{1,0:T(8,128)(2,1)} custom-call(bf16[16,4096]{1,0:T(8,128)(2,1)} %q_ref.1, bf16[16,4096]{1,0:T(8,128)(2,1)} %res_ref.1, bf16[16,256,256]{2,1,0:T(8,128)(2,1)} %kv_hbm.1, s32[16]{0:T(128)} %len_ref.1, s32[3,16]{1,0:T(4,128)} %bitcast.8, f32[3,16]{1,0:T(4,128)} %bitcast.9, f32[1,4096]{1,0:T(1,128)} %bitcast.7, ...), custom_call_target="tpu_custom_call" | custom-call | tf_op jit(solution)/shard_map/moe_step/pallas_call | solution.py:383
  66.5 1.6 %copy.11 = bf16[16,4096]{1,0:T(8,128)(2,1)} copy(bf16[16,4096]{1,0:T(8,128)(2,1)} %moe_step.1) | data formatting | bytes 262144

commit v4 on v3

--- a/solution.py
+++ b/solution.py
@@ -171,7 +171,7 @@
         return remote(disp.at[i], arr.at[i], d_send.at[i], d_recv.at[i], on_col(i, 1))
 
     def send(g):
-        for i in range(max(1, g * PER), (g + 1) * PER):
+        for i in reversed(range(max(1, g * PER), (g + 1) * PER)):
             start(d_copy, i)
 
     pl.semaphore_wait(barrier, COLS - 1 + 3)
@@ -340,7 +340,7 @@
                 ret[0] = piece
             else:
                 rsend[i] = piece
-        for i in range(max(1, g * PER), (g + 1) * PER):
+        for i in reversed(range(max(1, g * PER), (g + 1) * PER)):
             start(e_copy, i)
 
     def combine(g):

time: 68.2 us -> 67.9 us (level)
  no operation moved by 1% of the time
where the time goes in v4:
time: 67.9 us; the launch traced here: 67.8 us
  Pallas kernels  66.2 us (97%)
  local copies, waits for them, and re-layouts  1.57 us (2%)
    pallas_call x1, Pallas kernels, on_device(): pl.pallas_call(kernel, out_shape=jax.ShapeDtypeStruct((rows, width), BF16...  66.2 us
    unnamed x1, local copies, waits for them, and re-layouts  1.57 us

profile of v4, /device:TPU:2, one launch (start us, length us, event | category | flops | bytes accessed | tf_op | source)
XLA Modules:
  0.0 67.8 jit_solution(11599654092999683073)
XLA Ops:
  0.0 66.2 %moe_step.1 = bf16[16,4096]{1,0:T(8,128)(2,1)} custom-call(bf16[16,4096]{1,0:T(8,128)(2,1)} %q_ref.1, bf16[16,4096]{1,0:T(8,128)(2,1)} %res_ref.1, bf16[16,256,256]{2,1,0:T(8,128)(2,1)} %kv_hbm.1, s32[16]{0:T(128)} %len_ref.1, s32[3,16]{1,0:T(4,128)} %bitcast.8, f32[3,16]{1,0:T(4,128)} %bitcast.9, f32[1,4096]{1,0:T(1,128)} %bitcast.7, ...), custom_call_target="tpu_custom_call" | custom-call | tf_op jit(solution)/shard_map/moe_step/pallas_call | solution.py:383
  66.2 1.6 %copy.11 = bf16[16,4096]{1,0:T(8,128)(2,1)} copy(bf16[16,4096]{1,0:T(8,128)(2,1)} %moe_step.1) | data formatting | bytes 262144
